TPU v7x, 512 devices: a whole 4x8x8 slice. The times are simulated.
512 devices in a mesh: mem: 32 (over z, x), geo: 16 (over y, core).
Axes of the slice: x: 4, y: 8, z: 8, core: 2. Of those that a mesh axis runs over, the one named last changes fastest.
Arguments:
- control: float32 [32, 32, 48, 384], P('mem', 'geo'), may hold values from -6 to 6
- kappa_table: float32 [16], replicated, may hold values from 0.02 to 0.24
- kappa_index: int32 [48, 384], replicated, may hold values from 0 to 15
- tile_bounds: int32 [17], replicated, may hold values from 0 to 18432, as said below
- filter_bands: float32 [16, 5, 32], replicated, may hold values from -0.3 to 0.3
- perturbation: bfloat16 [2, 32, 32, 18432], P(None, 'mem', None, 'geo'), may hold values from -6 to 6
Outputs:
- increment: float32 [2, 32, 18432], P(None, 'mem', 'geo')
Inputs may be any that keep to these rules, and one draw needn't show every extreme that they name: tile_bounds[0] is 0, tile_bounds[16] is 18432, and the bounds never fall; tile t holds columns tile_bounds[t] to tile_bounds[t + 1] - 1.
All inputs are finite; a program needn't handle non-finite values.
Results may differ from a plain program's by a relative error of at most 0.005.
Values may be sent and summed in bfloat16 or wider, within the bound.
No kernel may reach another device: no remote copies, remote signals or barrier semaphores. Data moves between devices by JAX's collectives and lax.ppermute only.
A program may use at most 64 MiB of HBM per device.

v0:
```python
import jax
import jax.numpy as jnp
from jax import lax
from jax.sharding import PartitionSpec as P

ITERS = 10


def neighbours(state):
    east = jnp.concatenate([state[..., 1:, :], state[..., -1:, :]], axis=-2)
    west = jnp.concatenate([state[..., :1, :], state[..., :-1, :]], axis=-2)
    north = jnp.concatenate([state[..., 1:], state[..., -1:]], axis=-1)
    south = jnp.concatenate([state[..., :1], state[..., :-1]], axis=-1)
    return (east, west, north, south)


def face_weights(kappa_field):
    return tuple((0.5 * (kappa_field + other) for other in neighbours(kappa_field)))


def diffuse_step(state, weights):
    east, west, north, south = neighbours(state)
    update = weights[0] * (east - state) + weights[1] * (west - state)
    update = update + weights[2] * (north - state) + weights[3] * (south - state)
    return state + update


def vertical_filter(values, coefficients):
    levels = values.shape[0]
    padded = jnp.pad(values, ((2, 2), (0, 0)))
    result = values
    for offset in range(5):
        result = result + coefficients[offset] * padded[offset : offset + levels]
    return result


def body(control, kappa_table, kappa_index, tile_bounds, filter_bands, perturbation):
    kappa_field = jnp.zeros(kappa_index.shape, jnp.float32)
    for entry in range(kappa_table.shape[0]):
        kappa_field = kappa_field + jnp.where(kappa_index == entry, kappa_table[entry], 0.0)
    weights = face_weights(kappa_field)
    state_field = lax.fori_loop(0, ITERS, lambda step, cur: diffuse_step(cur, weights), control)
    flattened = state_field.reshape(state_field.shape[0], state_field.shape[1], -1)
    by_columns = lax.all_to_all(flattened, "geo", split_axis=2, concat_axis=1, tiled=True)
    width = by_columns.shape[2]
    tiles_count = filter_bands.shape[0]
    columns = lax.axis_index("geo") * width + jnp.arange(width, dtype=jnp.int32)
    tile_ids = jnp.sum((columns[None, :] >= tile_bounds[1:-1][:, None]).astype(jnp.int32), axis=0)
    one_hot = (tile_ids[None, :] == jnp.arange(tiles_count, dtype=jnp.int32)[:, None]).astype(
        jnp.float32
    )
    coefficients = jnp.einsum("tkl,tc->klc", filter_bands, one_hot, precision=lax.Precision.HIGHEST)
    filtered = vertical_filter(by_columns[0], coefficients).astype(jnp.bfloat16)
    products = perturbation[:, 0].astype(jnp.float32) * filtered.astype(jnp.float32)[None]
    return lax.psum_scatter(products, "mem", scatter_dimension=1, tiled=True)


def solution(mesh):
    in_specs = (P("mem", "geo", None, None), P(), P(), P(), P(), P(None, "mem", None, "geo"))
    out_specs = P(None, "mem", "geo")
    return jax.shard_map(body, mesh=mesh, in_specs=in_specs, out_specs=out_specs, check_vma=False)
```

profile of v0, /device:TPU:1, one launch (start us, length us, event | category | flops | bytes accessed | tf_op | source)
XLA Modules:
  0.0 337.4 jit_solution(5433511955447139947)
XLA Ops:
  6.5 0.9 copy.26
  7.5 1.9 fusion.35
  9.4 10.9 %select_add_fusion = f32[48,384]{1,0:T(8,128)S(1)} fusion(s32[48,384]{1,0:T(8,128)} %param.10, f32[]{:T(128)} %bitcast.16, f32[]{:T(128)} %bitcast.15, f32[]{:T(128)} %bitcast.14, f32[]{:T(128)} %bitcast.13, f32[]{:T(128)} %bitcast.12, f32[]{:T(128)} %bitcast.11, f32[]{:T(128)} %bitcast.10, f32[]{:T(128)} %bitcast.9, f32[]{:T(128)} %bitcast.8, f32[]{:T(128)} %bitcast.7, ...), kind=kLoop, calls=%fused_computation.44 | loop fusion | flops 866304 | bytes 147520 | tf_op jit(solution)/shard_map/add | solution.py:40
  20.5 11.0 %fusion.22 = (f32[48,384]{1,0:T(8,128)S(1)}, f32[48,384]{1,0:T(8,128)S(1)}, f32[48,384]{1,0:T(8,128)S(1)}, f32[48,384]{1,0:T(8,128)S(1)}) fusion(f32[48,383]{1,0:T(8,128)S(1)} %get-tuple-element.64, f32[48,1]{1,0:T(8,128)S(1)} %get-tuple-element.62, f32[48,1]{1,0:T(8,128)S(1)} %get-tuple-element.63, f32[48,383]{1,0:T(8,128)S(1)} %get-tuple-element.65, ...), kind=kLoop, calls=%fused_computation.41 | loop fusion | flops 1087488 | bytes 663616 | tf_op jit(solution)/shard_map/mul | solution.py:18
  31.5 4.1 %while.10 = (s32[]{:T(128)}, f32[1,2,48,384]{3,2,1,0:T(8,128)S(1)}, f32[48,384]{1,0:T(8,128)S(1)}, f32[48,384]{1,0:T(8,128)S(1)}, f32[48,384]{1,0:T(8,128)S(1)}, /*index=5*/f32[48,384]{1,0:T(8,128)S(1)}, s32[]{:T(128)}) while((s32[]{:T(128)}, f32[1,2,48,384]{3,2,1,0:T(8,128)S(1)}, f32[48,384]{1,0:T(8,128)S(1)}, f32[48,384]{1,0:T(8,128)S(1)}, ...), condition=%wide.region_1.2_spmd, body=%wide.region_0.1_spmd.sunk | while | flops 589826 | bytes 2359373 | solution.py:42
  32.1 0.2 fusion.46
  33.8 0.2 fusion.46
  35.0 0.2 fusion.46
  35.6 5.6 %copy.13 = f32[1,2,48,384]{1,3,2,0:T(8,128)} copy(f32[1,2,48,384]{3,2,1,0:T(8,128)S(1)} %get-tuple-element.37) | data formatting | bytes 294912 | tf_op jit(solution)/shard_map/while | solution.py:42
  41.2 0.5 broadcast.25
  41.7 83.6 %reduce = f32[18432,2]{1,0:T(8,128)} reduce(f32[18432,1,2]{2,1,0:T(1,128)} %bitcast.63, f32[]{:T(128)} %broadcast.25), dimensions={1}, to_apply=%bitcast.60.reduce_sub_computation | reduce | bytes 294916
  125.3 8.9 %reshape.29 = f32[16,1,2304]{2,1,0:T(1,128)} reshape(f32[18432,2]{1,0:T(8,128)} %reduce) | data formatting | bytes 294912
  134.1 10.2 %all-to-all-start = ((f32[16,1,2304]{2,1,0:T(1,128)}), f32[16,1,2304]{2,1,0:T(1,128)S(1)}, u32[]{:S(2)}, u32[]{:S(2)}) async-start(f32[16,1,2304]{2,1,0:T(1,128)} %reshape.29), calls=%async_computation | async-start | bytes 294912 | tf_op jit(solution)/shard_map/all_to_all | solution.py:44
  144.3 0.2 all-reduce.4.cloned.1.call-start
  144.8 0.5 convolution_bitcast_fusion
  145.3 8.6 %all-to-all-done = f32[16,1,2304]{2,1,0:T(1,128)S(1)} async-done(((f32[16,1,2304]{2,1,0:T(1,128)}), f32[16,1,2304]{2,1,0:T(1,128)S(1)}, u32[]{:S(2)}, u32[]{:S(2)}) %all-to-all-start) | async-done | bytes 147488 | tf_op jit(solution)/shard_map/all_to_all | solution.py:44
  153.9 1.0 reduce.1
  154.9 17.8 %reshape.30 = f32[18432,1,2]{2,1,0:T(1,128)} reshape(f32[16,2304]{1,0:T(8,128)S(1)} %reduce.1) | data formatting | bytes 294912
  172.7 5.6 %copy.14 = f32[1,2,16,1152]{3,1,2,0:T(2,128)S(1)} copy(f32[1,2,16,1152]{1,3,2,0:T(8,128)} %bitcast.64) | data formatting | bytes 294912 | tf_op jit(solution)/shard_map/all_to_all | solution.py:44
  178.6 0.9 convert_multiply_fusion
  179.5 1.3 dynamic-slice
  180.7 147.9 %all-reduce.4.cloned.1.call-done = f32[2,32,1152]{2,0,1:T(2,128)} async-done(((f32[2,32,1152]{2,0,1:T(2,128)}), f32[2,32,1152]{2,0,1:T(2,128)}) %all-reduce.4.cloned.1.call-update) | async-done | bytes 294928
  328.6 1.3 constant_dynamic-slice_fusion
  329.9 0.6 copy.15
  (63 shorter events, 3.7 us)
Async XLA Ops:
  6.5 138.2 %copy-start = (f32[16,5,32]{2,0,1:T(8,128)S(1)}, f32[16,5,32]{2,0,1:T(8,128)}, u32[]{:S(2)}) copy-start(f32[16,5,32]{2,0,1:T(8,128)} %param.12) | copy-start | bytes 30724
  125.2 19.3 %copy-start.2 = (s32[17]{0:T(128)S(1)}, s32[17]{0:T(128)}, u32[]{:S(2)}) copy-start(s32[17]{0:T(128)} %param.11) | copy-start | bytes 208
  134.1 19.7 %all-to-all-start = ((f32[16,1,2304]{2,1,0:T(1,128)}), f32[16,1,2304]{2,1,0:T(1,128)S(1)}, u32[]{:S(2)}, u32[]{:S(2)}) async-start(f32[16,1,2304]{2,1,0:T(1,128)} %reshape.29), calls=%async_computation | async-start | bytes 294912 | tf_op jit(solution)/shard_map/all_to_all | solution.py:44
  144.3 184.3 %all-reduce.4.cloned.1.call-start = ((), (), s32[]{:S(2)}) async-start(), calls=%async_computation.1 | async-start | bytes 589824
  154.9 23.7 %copy-start.1 = (bf16[2,1,32,1152]{3,2,1,0:T(8,128)(2,1)S(1)}, bf16[2,1,32,1152]{3,2,1,0:T(8,128)(2,1)}, u32[]{:S(2)}) copy-start(bf16[2,1,32,1152]{3,2,1,0:T(8,128)(2,1)} %param.13) | copy-start | bytes 442372
Sparse Core Ops, SparseCore 0:
  179.6 148.9 all-reduce.3
where the time goes:
time: 342 us; the launch traced here: 337 us
  waiting for transfers between devices  156 us (46%)
  other arithmetic  109 us (32%)
  local copies, waits for them, and re-layouts  47 us (14%)
  between operations  13.5 us (4%)
  starting transfers between devices  10.4 us (3%)
    unnamed x2, waiting for transfers between devices  148 us
    unnamed x1, other arithmetic  83.6 us
    unnamed x12, local copies, waits for them, and re-layouts  30.8 us
    mul x1, other arithmetic, face_weights(): 0.5 * (kappa_field + other)  11 us
    add x1, other arithmetic, body(): kappa_field + jnp.where(kappa_index == entry, kappa_table[entry], 0.0)  10.9 us
    all_to_all x1, starting transfers between devices, body(): lax.all_to_all(flattened, 'geo', split_axis=2, concat_axis=1, tiled=True)  10.2 us
    all_to_all x1, waiting for transfers between devices, body(): lax.all_to_all(flattened, 'geo', split_axis=2, concat_axis=1, tiled=True)  8.62 us
  transfers between devices with their start and end apart: 2, of which 2 were waited for; matrix products, arithmetic and copies ran while one was open for 1% of the time, Pallas kernels for 0%

commit v1 on v0

v1 whole, which is shorter than its diff:
```python
import jax
import jax.numpy as jnp
from jax import lax
from jax.experimental import pallas as pl
from jax.experimental.pallas import tpu as pltpu
from jax.sharding import PartitionSpec as P

ITERS = 10
LANES = 128
VMEM = pl.BlockSpec(memory_space=pltpu.VMEM)
SMEM = pl.BlockSpec(memory_space=pltpu.SMEM)


def diffuse_kernel(control_ref, table_ref, index_ref, out_ref, rows_ref):
    levels, height, width = control_ref.shape[1:]
    groups = out_ref.shape[0]
    phases = height // groups
    lane_tiles = width // LANES

    def phase(load, r):
        for k in range(lane_tiles):
            rows_ref[k] = load(k)
        return [rows_ref[k, pl.ds(r, groups, stride=phases), :] for k in range(lane_tiles)]

    def split(load):
        for k in range(lane_tiles):
            rows_ref[k] = load(k)
        return [
            jnp.concatenate(
                [rows_ref[k, pl.ds(r, groups, stride=phases), :] for k in range(lane_tiles)], axis=1
            )
            for r in range(phases)
        ]

    def kappa_tile(k):
        index = index_ref[:, k * LANES : (k + 1) * LANES]
        value = jnp.zeros(index.shape, jnp.float32)
        for entry in range(table_ref.shape[0]):
            value = jnp.where(index == entry, table_ref[entry], value)
        return value

    def right(x):
        return pltpu.roll(x, width - 1, 1)

    def left(x):
        return pltpu.roll(x, 1, 1)

    def down(x):
        return pltpu.roll(x, groups - 1, 0)

    def up(x):
        return pltpu.roll(x, 1, 0)

    kappa = split(kappa_tile)
    column = lax.broadcasted_iota(jnp.int32, (groups, width), 1)
    group = lax.broadcasted_iota(jnp.int32, (groups, width), 0)
    north = [jnp.where(column < width - 1, 0.5 * (k + right(k)), 0.0) for k in kappa]
    east = [0.5 * (kappa[r] + kappa[r + 1]) for r in range(phases - 1)]
    last = 0.5 * (kappa[phases - 1] + down(kappa[0]))
    east.append(jnp.where(group < groups - 1, last, 0.0))

    for level in range(levels):
        state = split(lambda k: control_ref[0, level, :, k * LANES : (k + 1) * LANES])
        for step in range(ITERS):
            flux_n = [north[r] * (right(state[r]) - state[r]) for r in range(phases)]
            after = state[1:] + [down(state[0])]
            flux_e = [east[r] * (after[r] - state[r]) for r in range(phases)]
            before = [up(flux_e[phases - 1])] + flux_e[:-1]
            state = [
                state[r] + (flux_e[r] - before[r]) + (flux_n[r] - left(flux_n[r]))
                for r in range(phases)
            ]
        for r in range(phases):
            value = state[r].astype(jnp.bfloat16)
            out_ref[:, level, r * width : (r + 1) * width] = value


def diffuse(control, table, index, groups):
    levels, height, width = control.shape[1:]
    return pl.pallas_call(
        diffuse_kernel,
        out_shape=jax.ShapeDtypeStruct((groups, levels, height * width // groups), jnp.bfloat16),
        in_specs=[VMEM, SMEM, VMEM],
        out_specs=VMEM,
        scratch_shapes=[pltpu.VMEM((width // LANES, height, LANES), jnp.float32)],
        name="diffuse",
    )(control, table, index)


def product_kernel(state_ref, coef_ref, pert_ref, out_ref, pad_ref):
    shards, share, width = state_ref.shape
    levels = shards * share
    tiles = width // LANES
    bands = coef_ref.shape[0]
    margin = 8
    for c in range(tiles):
        lanes = slice(c * LANES, (c + 1) * LANES)
        pad_ref[c, 0:margin] = jnp.zeros((margin, LANES), jnp.float32)
        pad_ref[c, margin + levels : 2 * margin + levels] = jnp.zeros((margin, LANES), jnp.float32)
        for g in range(shards):
            pad_ref[c, margin + g * share : margin + (g + 1) * share] = state_ref[g, :, lanes].astype(jnp.float32)
        value = pad_ref[c, margin : margin + levels]
        for k in range(bands):
            start = margin + k - bands // 2
            value = value + coef_ref[k, :, lanes] * pad_ref[c, start : start + levels]
        for v in range(2):
            product = pert_ref[v, 0, :, lanes].astype(jnp.float32) * value
            out_ref[:, v, lanes] = product.astype(jnp.bfloat16)


def products(state, coefficients, perturbation):
    shards, share, width = state.shape
    levels = shards * share
    return pl.pallas_call(
        product_kernel,
        out_shape=jax.ShapeDtypeStruct((levels, 2, width), jnp.bfloat16),
        in_specs=[VMEM, VMEM, VMEM],
        out_specs=VMEM,
        scratch_shapes=[pltpu.VMEM((width // LANES, levels + 16, LANES), jnp.float32)],
        name="products",
    )(state, coefficients, perturbation)


def sum_kernel(terms_ref, out_ref):
    total = terms_ref[0].astype(jnp.float32)
    for m in range(1, terms_ref.shape[0]):
        total = total + terms_ref[m].astype(jnp.float32)
    for v in range(2):
        out_ref[v] = total[v : v + 1]


def total(terms):
    return pl.pallas_call(
        sum_kernel,
        out_shape=jax.ShapeDtypeStruct((terms.shape[1], 1, terms.shape[2]), jnp.float32),
        in_specs=[VMEM],
        out_specs=VMEM,
        name="total",
    )(terms)


def coefficients_of(tile_bounds, filter_bands, width):
    tiles = filter_bands.shape[0]
    columns = lax.axis_index("geo") * width + jnp.arange(width, dtype=jnp.int32)
    tile_ids = jnp.sum((columns[None, :] >= tile_bounds[1:-1][:, None]).astype(jnp.int32), axis=0)
    one_hot = (tile_ids[None, :] == jnp.arange(tiles, dtype=jnp.int32)[:, None]).astype(jnp.float32)
    return jnp.einsum("tkl,tc->klc", filter_bands, one_hot, precision=lax.Precision.HIGHEST)


def solution(mesh):
    groups = mesh.shape["geo"]

    def body(control, kappa_table, kappa_index, tile_bounds, filter_bands, perturbation):
        sent = diffuse(control, kappa_table, kappa_index, groups)
        state = lax.all_to_all(sent, "geo", 0, 0, tiled=True)
        coefficients = coefficients_of(tile_bounds, filter_bands, state.shape[2])
        terms = products(state, coefficients, perturbation)
        return total(lax.all_to_all(terms, "mem", 0, 0, tiled=True))

    in_specs = (P("mem", "geo", None, None), P(), P(), P(), P(), P(None, "mem", None, "geo"))
    out_specs = P(None, "mem", "geo")
    return jax.shard_map(body, mesh=mesh, in_specs=in_specs, out_specs=out_specs, check_vma=False)
```

time: 342 us -> 47.7 us (0.14); the launches traced: 337 us -> 47.4 us
  waiting for transfers between devices: 156 us -> 5.83 us
  other arithmetic: 109 us -> 0.1 us
  local copies, waits for them, and re-layouts: 47 us -> 1.36 us
  blocking collectives: 0 us -> 21.5 us
  between operations: 13.5 us -> 0.02 us
  Pallas kernels: 0 us -> 7.05 us
    unnamed x2 -> x0, waiting for transfers between devices: 148 us -> none
    unnamed x1 -> x0, other arithmetic: 83.6 us -> none
    unnamed x12 -> x6, local copies, waits for them, and re-layouts: 30.8 us -> 1.28 us
    all_to_all x0 -> x1, blocking collectives: none -> 21.5 us  [body(): return total(lax.all_to_all(terms, 'mem', 0, 0, tiled=True))]
    add x12 -> x1, other arithmetic: 12.5 us -> 0.01 us  [coefficients_of(): columns = lax.axis_index('geo') * width + jnp.arange(width, dtype=jnp.int32)]
    mul x2 -> x0, other arithmetic: 11.8 us -> none  [the longest x1 11 us: face_weights(): 0.5 * (kappa_field + other)]
    pallas_call x0 -> x3, Pallas kernels: none -> 7.05 us  [the longest x1 3.24 us: diffuse(): pl.pallas_call(diffuse_kernel, out_shape=jax.ShapeDtypeStruct((groups, le...]
    while x1 -> x0, local copies, waits for them, and re-layouts: 5.61 us -> none  [body(): lax.fori_loop(0, ITERS, lambda step, cur: diffuse_step(cur, weights), con...]
  transfers between devices with their start and end apart: 2 -> 1, of which waited for: 2 -> 1; matrix products, arithmetic and copies ran while one was open for 1% -> 3% of each run, Pallas kernels for 0% -> 0%
where the time goes in v1:
time: 47.7 us; the launch traced here: 47.4 us
  blocking collectives  21.5 us (45%)
  starting transfers between devices  10.2 us (21%)
  Pallas kernels  7.05 us (15%)
  waiting for transfers between devices  5.83 us (12%)
  local copies, waits for them, and re-layouts  1.36 us (3%)
  matrix products  1.36 us (3%)
    all_to_all x1, blocking collectives, body(): return total(lax.all_to_all(terms, 'mem', 0, 0, tiled=True))  21.5 us
    all_to_all x1, starting transfers between devices, body(): state = lax.all_to_all(sent, 'geo', 0, 0, tiled=True)  10.2 us
    all_to_all x1, waiting for transfers between devices, body(): state = lax.all_to_all(sent, 'geo', 0, 0, tiled=True)  5.83 us
    pallas_call x1, Pallas kernels, diffuse(): pl.pallas_call(diffuse_kernel, out_shape=jax.ShapeDtypeStruct((groups, le...  3.24 us
    pallas_call x1, Pallas kernels, products(): pl.pallas_call(product_kernel, out_shape=jax.ShapeDtypeStruct((levels, 2,...  2.26 us
    pallas_call x1, Pallas kernels, total(): pl.pallas_call(sum_kernel, out_shape=jax.ShapeDtypeStruct((terms.shape[1]...  1.55 us
    dot_general x1, matrix products, coefficients_of(): jnp.einsum('tkl,tc->klc', filter_bands, one_hot, precision=lax.Precision....  1.36 us
    unnamed x6, local copies, waits for them, and re-layouts  1.28 us
  transfers between devices with their start and end apart: 1, of which 1 were waited for; matrix products, arithmetic and copies ran while one was open for 3% of the time, Pallas kernels for 0%

profile of v1, /device:TPU:1, one launch (start us, length us, event | category | flops | bytes accessed | tf_op | source)
XLA Modules:
  0.0 47.4 jit_solution(10705737743907599075)
XLA Ops:
  0.0 0.0 copy-start
  0.0 3.2 %diffuse.1 = bf16[16,2,1152]{2,1,0:T(2,128)(2,1)} custom-call(f32[1,2,48,384]{3,2,1,0:T(8,128)} %control_ref.1, f32[16]{0:T(128)} %table_ref.1, s32[48,384]{1,0:T(8,128)} %index_ref.1), custom_call_target="tpu_custom_call" | custom-call | tf_op jit(solution)/shard_map/diffuse/pallas_call | solution.py:80
  3.2 10.2 %all-to-all-start = ((bf16[16,2,1152]{2,1,0:T(2,128)(2,1)}), bf16[16,2,1152]{2,1,0:T(2,128)(2,1)S(1)}, u32[]{:S(2)}, u32[]{:S(2)}) async-start(bf16[16,2,1152]{2,1,0:T(2,128)(2,1)} %diffuse.1), calls=%async_computation | async-start | bytes 147456 | tf_op jit(solution)/shard_map/all_to_all | solution.py:155
  13.4 0.0 copy-start.2
  13.4 0.6 %copy-done.2 = s32[17]{0:T(128)S(1)} copy-done((s32[17]{0:T(128)S(1)}, s32[17]{0:T(128)}, u32[]{:S(2)}) %copy-start.2) | copy-done | bytes 92
  14.1 0.1 slice.3
  14.1 0.1 convert_reduce_fusion
  14.2 0.0 copy-done
  14.3 1.4 %convolution_bitcast_fusion.coef_ref = f32[5,32,1152]{2,1,0:T(8,128)} fusion(f32[16,5,32]{2,0,1:T(8,128)S(1)} %copy-done, s32[1152]{0:T(1024)S(1)} %convert_reduce_fusion), kind=kOutput, calls=%fused_computation | convolution fusion | flops 35407872 | bytes 752128 | tf_op jit(solution)/shard_map/tkl,tc->klc/dot_general | solution.py:147
  15.6 5.8 %all-to-all-done.state_ref = bf16[16,2,1152]{2,1,0:T(2,128)(2,1)S(1)} async-done(((bf16[16,2,1152]{2,1,0:T(2,128)(2,1)}), bf16[16,2,1152]{2,1,0:T(2,128)(2,1)S(1)}, u32[]{:S(2)}, u32[]{:S(2)}) %all-to-all-start) | async-done | bytes 73760 | tf_op jit(solution)/shard_map/all_to_all | solution.py:155
  21.4 0.0 copy-start.1
  21.4 0.6 %copy-done.1 = bf16[16,2,1152]{2,1,0:T(2,128)(2,1)} copy-done((bf16[16,2,1152]{2,1,0:T(2,128)(2,1)}, bf16[16,2,1152]{2,1,0:T(2,128)(2,1)S(1)}, u32[]{:S(2)}) %copy-start.1) | copy-done | bytes 73752
  22.1 2.3 %products.1 = bf16[32,2,1152]{2,1,0:T(2,128)(2,1)} custom-call(bf16[16,2,1152]{2,1,0:T(2,128)(2,1)} %copy-done.1, f32[5,32,1152]{2,1,0:T(8,128)} %convolution_bitcast_fusion.coef_ref, bf16[2,1,32,1152]{3,2,1,0:T(8,128)(2,1)} %pert_ref.1), custom_call_target="tpu_custom_call" | custom-call | tf_op jit(solution)/shard_map/products/pallas_call | solution.py:114
  24.3 21.5 %all_to_all.10.terms_ref = bf16[32,2,1152]{2,1,0:T(2,128)(2,1)} all-to-all(bf16[32,2,1152]{2,1,0:T(2,128)(2,1)} %products.1), channel_id=1, replica_groups=mesh['mem'=32,'geo'=16] {'mem'}, dimensions={0} | all-to-all | bytes 294912 | tf_op jit(solution)/shard_map/all_to_all | solution.py:158
  45.9 1.5 %total.1 = f32[2,1,1152]{2,1,0:T(1,128)} custom-call(bf16[32,2,1152]{2,1,0:T(2,128)(2,1)} %all_to_all.10.terms_ref), custom_call_target="tpu_custom_call" | custom-call | tf_op jit(solution)/shard_map/total/pallas_call | solution.py:133
  (1 shorter events, 0.0 us)
Async XLA Ops:
  0.0 14.2 %copy-start = (f32[16,5,32]{2,0,1:T(8,128)S(1)}, f32[16,5,32]{2,0,1:T(8,128)}, u32[]{:S(2)}) copy-start(f32[16,5,32]{2,0,1:T(8,128)} %param.10) | copy-start | bytes 30724
  3.2 18.2 %all-to-all-start = ((bf16[16,2,1152]{2,1,0:T(2,128)(2,1)}), bf16[16,2,1152]{2,1,0:T(2,128)(2,1)S(1)}, u32[]{:S(2)}, u32[]{:S(2)}) async-start(bf16[16,2,1152]{2,1,0:T(2,128)(2,1)} %diffuse.1), calls=%async_computation | async-start | bytes 147456 | tf_op jit(solution)/shard_map/all_to_all | solution.py:155
  13.4 0.7 %copy-start.2 = (s32[17]{0:T(128)S(1)}, s32[17]{0:T(128)}, u32[]{:S(2)}) copy-start(s32[17]{0:T(128)} %param.9) | copy-start | bytes 208
  21.4 0.6 %copy-start.1 = (bf16[16,2,1152]{2,1,0:T(2,128)(2,1)}, bf16[16,2,1152]{2,1,0:T(2,128)(2,1)S(1)}, u32[]{:S(2)}) copy-start(bf16[16,2,1152]{2,1,0:T(2,128)(2,1)S(1)} %all-to-all-done.state_ref) | copy-start | bytes 221188

commit v2 on v1

v2 whole, which is shorter than its diff:
```python
import jax
import jax.numpy as jnp
from jax import lax
from jax.experimental import pallas as pl
from jax.experimental.pallas import tpu as pltpu
from jax.sharding import PartitionSpec as P

ITERS = 10
LANES = 128
HBM = pl.BlockSpec(memory_space=pltpu.HBM)
VMEM = pl.BlockSpec(memory_space=pltpu.VMEM)
SMALL = pltpu.CompilerParams(vmem_limit_bytes=4 << 20)


def coefficients(bounds_ref, bands_ref, out_ref):
    tiles = bands_ref.shape[1]
    width = out_ref.shape[2]
    first = lax.axis_index("geo") * width
    column = first + lax.broadcasted_iota(jnp.int32, (tiles, width), 1)
    tile = jnp.zeros((tiles, width), jnp.int32)
    for j in range(1, tiles):
        tile = tile + (column >= bounds_ref[j]).astype(jnp.int32)
    own = (tile == lax.broadcasted_iota(jnp.int32, (tiles, width), 0)).astype(jnp.float32)
    own = own.astype(jnp.bfloat16)
    for k in range(out_ref.shape[0]):
        rest = bands_ref[k]
        value = 0.0
        for part in range(3):
            piece = rest.astype(jnp.bfloat16)
            rest = rest - piece.astype(jnp.float32)
            value = value + lax.dot_general(
                piece, own, (((0,), (0,)), ((), ())), preferred_element_type=jnp.float32
            )
        out_ref[k] = value


def diffuse_kernel(
    control_hbm,
    table_hbm,
    index_hbm,
    bounds_hbm,
    bands_hbm,
    out_ref,
    coef_ref,
    control_ref,
    table_ref,
    index_ref,
    bounds_ref,
    bands_ref,
    rows_ref,
    sems,
):
    copies = [
        pltpu.make_async_copy(source, target, sems.at[i])
        for i, (source, target) in enumerate(
            (
                (bounds_hbm, bounds_ref),
                (bands_hbm, bands_ref),
                (table_hbm, table_ref),
                (index_hbm, index_ref),
                (control_hbm, control_ref),
            )
        )
    ]
    for copy in copies:
        copy.start()
    levels, height, width = control_ref.shape[1:]
    groups = out_ref.shape[0]
    phases = height // groups
    tiles = width // LANES
    each = range(phases)

    def split(slot, load):
        for k in range(tiles):
            rows_ref[slot, k] = load(slice(k * LANES, (k + 1) * LANES))
        return [
            jnp.concatenate(
                [rows_ref[slot, k, pl.ds(r, groups, stride=phases), :] for k in range(tiles)],
                axis=1,
            )
            for r in each
        ]

    def kappa_of(lanes):
        index = index_ref[:, lanes]
        values = [table_ref[entry] for entry in range(table_ref.shape[0])]
        bit = 1
        while len(values) > 1:
            odd = (index & bit) != 0
            values = [jnp.where(odd, b, a) for a, b in zip(values[::2], values[1::2])]
            bit *= 2
        return values[0]

    def north_of(x):
        return pltpu.roll(x, width - 1, 1)

    def south_of(x):
        return pltpu.roll(x, 1, 1)

    def next_group(x):
        return pltpu.roll(x, groups - 1, 0)

    def previous_group(x):
        return pltpu.roll(x, 1, 0)

    copies[0].wait()
    copies[1].wait()
    coefficients(bounds_ref, bands_ref, coef_ref)
    copies[2].wait()
    copies[3].wait()
    kappa = split(levels, kappa_of)
    column = lax.broadcasted_iota(jnp.int32, (groups, width), 1)
    group = lax.broadcasted_iota(jnp.int32, (groups, width), 0)
    north = [jnp.where(column < width - 1, 0.5 * (k + north_of(k)), 0.0) for k in kappa]
    south = [south_of(w) for w in north]
    east = [0.5 * (kappa[r] + kappa[r + 1]) for r in range(phases - 1)]
    last = 0.5 * (kappa[-1] + next_group(kappa[0]))
    east.append(jnp.where(group < groups - 1, last, 0.0))
    west = [previous_group(east[-1])] + east[:-1]
    own = [1.0 - ((east[r] + west[r]) + (north[r] + south[r])) for r in each]

    def step(state):
        after = state[1:] + [next_group(state[0])]
        before = [previous_group(state[-1])] + state[:-1]
        return [
            (own[r] * state[r] + (east[r] * after[r] + west[r] * before[r]))
            + (north[r] * north_of(state[r]) + south[r] * south_of(state[r]))
            for r in each
        ]

    copies[4].wait()
    states = [split(v, lambda lanes: control_ref[0, v, :, lanes]) for v in range(levels)]
    for _ in range(ITERS):
        states = [step(state) for state in states]
    for level in range(levels):
        for r in each:
            value = states[level][r].astype(jnp.bfloat16)
            out_ref[:, level, r * width : (r + 1) * width] = value


def diffuse(control, table, index, bounds, bands, groups):
    levels, height, width = control.shape[1:]
    share = height * width // groups
    arguments = [
        pltpu.with_memory_space_constraint(x, pltpu.HBM)
        for x in (control, table, index, bounds, bands)
    ]
    return pl.pallas_call(
        diffuse_kernel,
        out_shape=(
            jax.ShapeDtypeStruct((groups, levels, share), jnp.bfloat16),
            jax.ShapeDtypeStruct((bands.shape[0], bands.shape[2], share), jnp.float32),
        ),
        in_specs=[HBM] * 5,
        out_specs=(VMEM, VMEM),
        scratch_shapes=[
            pltpu.VMEM(control.shape, jnp.float32),
            pltpu.SMEM(table.shape, jnp.float32),
            pltpu.VMEM(index.shape, jnp.int32),
            pltpu.SMEM(bounds.shape, jnp.int32),
            pltpu.VMEM(bands.shape, jnp.float32),
            pltpu.VMEM((levels + 1, width // LANES, height, LANES), jnp.float32),
            pltpu.SemaphoreType.DMA((5,)),
        ],
        compiler_params=SMALL,
        name="diffuse",
    )(*arguments)


def product_kernel(state_ref, coef_ref, pert_ref, out_ref, pad_ref):
    shards, share, width = state_ref.shape
    levels = shards * share
    bands = coef_ref.shape[0]
    margin = 8
    for c in range(width // LANES):
        lanes = slice(c * LANES, (c + 1) * LANES)
        pad_ref[c, 0:margin] = jnp.zeros((margin, LANES), jnp.float32)
        pad_ref[c, margin + levels : 2 * margin + levels] = jnp.zeros((margin, LANES), jnp.float32)
        for g in range(shards):
            rows = slice(margin + g * share, margin + (g + 1) * share)
            pad_ref[c, rows] = state_ref[g, :, lanes].astype(jnp.float32)
        value = pad_ref[c, margin : margin + levels]
        for k in range(bands):
            start = margin + k - bands // 2
            value = value + coef_ref[k, :, lanes] * pad_ref[c, start : start + levels]
        for v in range(2):
            product = pert_ref[v, 0, :, lanes].astype(jnp.float32) * value
            out_ref[:, v, lanes] = product.astype(jnp.bfloat16)


def products(state, coefs, perturbation):
    shards, share, width = state.shape
    levels = shards * share
    return pl.pallas_call(
        product_kernel,
        out_shape=jax.ShapeDtypeStruct((levels, 2, width), jnp.bfloat16),
        in_specs=[VMEM, VMEM, VMEM],
        out_specs=VMEM,
        scratch_shapes=[pltpu.VMEM((width // LANES, levels + 16, LANES), jnp.float32)],
        compiler_params=SMALL,
        name="products",
    )(state, coefs, perturbation)


def sum_kernel(terms_ref, out_ref):
    total = terms_ref[0].astype(jnp.float32)
    for m in range(1, terms_ref.shape[0]):
        total = total + terms_ref[m].astype(jnp.float32)
    for v in range(2):
        out_ref[v] = total[v : v + 1]


def member_sum(terms):
    return pl.pallas_call(
        sum_kernel,
        out_shape=jax.ShapeDtypeStruct((terms.shape[1], 1, terms.shape[2]), jnp.float32),
        in_specs=[VMEM],
        out_specs=VMEM,
        compiler_params=SMALL,
        name="member_sum",
    )(terms)


def solution(mesh):
    groups = mesh.shape["geo"]

    def body(control, kappa_table, kappa_index, tile_bounds, filter_bands, perturbation):
        bands = jnp.transpose(filter_bands, (1, 0, 2))
        sent, coefs = diffuse(control, kappa_table, kappa_index, tile_bounds, bands, groups)
        state = lax.all_to_all(sent, "geo", 0, 0, tiled=True)
        terms = products(state, coefs, perturbation)
        return member_sum(lax.all_to_all(terms, "mem", 0, 0, tiled=True))

    in_specs = (P("mem", "geo", None, None), P(), P(), P(), P(), P(None, "mem", None, "geo"))
    out_specs = P(None, "mem", "geo")
    return jax.shard_map(body, mesh=mesh, in_specs=in_specs, out_specs=out_specs, check_vma=False)
```

time: 47.7 us -> 43.1 us (0.904)
  blocking collectives: 21.5 us -> 39.2 us
  starting transfers between devices: 10.2 us -> 0 us
  waiting for transfers between devices: 5.83 us -> 0 us
  Pallas kernels: 7.05 us -> 3.65 us
  matrix products: 1.36 us -> 0 us
  local copies, waits for them, and re-layouts: 1.36 us -> 0.01 us
    all_to_all x1 -> x2, blocking collectives: 21.5 us -> 39.2 us  [the longest x1 21.9 us: body(): return member_sum(lax.all_to_all(terms, 'mem', 0, 0, tiled=True))]
    all_to_all x1 -> x0, starting transfers between devices: 10.2 us -> none  [body(): state = lax.all_to_all(sent, 'geo', 0, 0, tiled=True)]
    all_to_all x1 -> x0, waiting for transfers between devices: 5.83 us -> none  [body(): state = lax.all_to_all(sent, 'geo', 0, 0, tiled=True)]
    pallas_call x1, Pallas kernels: 2.26 us -> 0.45 us  [products(): pl.pallas_call(product_kernel, out_shape=jax.ShapeDtypeStruct((levels, 2,...]
    pallas_call x2, Pallas kernels: 4.79 us -> 3.2 us  [the longest x1 2.55 us: diffuse(): pl.pallas_call(diffuse_kernel, out_shape=(jax.ShapeDtypeStruct((groups, l...]
    dot_general x1 -> x0, matrix products: 1.36 us -> none  [coefficients_of(): jnp.einsum('tkl,tc->klc', filter_bands, one_hot, precision=lax.Precision....]
    unnamed x6 -> x2, local copies, waits for them, and re-layouts: 1.28 us -> 0.01 us
  transfers between devices with their start and end apart: 1 -> 0, of which waited for: 1 -> 0; matrix products, arithmetic and copies ran while one was open for 3% -> 0% of each run, Pallas kernels for 0% -> 0%
where the time goes in v2:
time: 43.1 us; the launch traced here: 42.9 us
  blocking collectives  39.2 us (91%)
  Pallas kernels  3.65 us (8%)
    all_to_all x1, blocking collectives, body(): return member_sum(lax.all_to_all(terms, 'mem', 0, 0, tiled=True))  21.9 us
    all_to_all x1, blocking collectives, body(): state = lax.all_to_all(sent, 'geo', 0, 0, tiled=True)  17.3 us
    pallas_call x1, Pallas kernels, diffuse(): pl.pallas_call(diffuse_kernel, out_shape=(jax.ShapeDtypeStruct((groups, l...  2.55 us

profile of v2, /device:TPU:1, one launch (start us, length us, event | category | flops | bytes accessed | tf_op | source)
XLA Modules:
  0.0 42.9 jit_solution(16455192004316930041)
XLA Ops:
  0.0 0.0 copy-start
  0.0 2.6 %diffuse.1 = (bf16[16,2,1152]{2,1,0:T(2,128)(2,1)S(1)}, f32[5,32,1152]{2,1,0:T(8,128)S(1)}) custom-call(f32[1,2,48,384]{3,2,1,0:T(8,128)} %control_hbm.1, f32[16]{0:T(128)} %table_hbm.1, s32[48,384]{1,0:T(8,128)} %index_hbm.1, s32[17]{0:T(128)} %bounds_hbm.1, f32[5,16,32]{2,1,0:T(8,128)} %bitcast.1), custom_call_target="tpu_custom_call" | custom-call | tf_op jit(solution)/shard_map/diffuse/pallas_call | solution.py:148
  2.6 17.3 %all_to_all.10.state_ref = bf16[16,2,1152]{2,1,0:T(2,128)(2,1)S(1)} all-to-all(bf16[16,2,1152]{2,1,0:T(2,128)(2,1)S(1)} %get-tuple-element.7), channel_id=1, replica_groups=mesh['mem'=32,'geo'=16] {'geo'}, dimensions={0} | all-to-all | bytes 147456 | tf_op jit(solution)/shard_map/all_to_all | solution.py:230
  19.9 0.0 copy-done
  19.9 0.5 %products.1 = bf16[32,2,1152]{2,1,0:T(2,128)(2,1)S(1)} custom-call(bf16[16,2,1152]{2,1,0:T(2,128)(2,1)S(1)} %all_to_all.10.state_ref, f32[5,32,1152]{2,1,0:T(8,128)S(1)} %get-tuple-element.8.coef_ref, bf16[2,1,32,1152]{3,2,1,0:T(8,128)(2,1)S(1)} %copy-done), custom_call_target="tpu_custom_call" | custom-call | tf_op jit(solution)/shard_map/products/pallas_call | solution.py:194
  20.3 21.9 %all_to_all.11.terms_ref = bf16[32,2,1152]{2,1,0:T(2,128)(2,1)S(1)} all-to-all(bf16[32,2,1152]{2,1,0:T(2,128)(2,1)S(1)} %products.1), channel_id=1, replica_groups=mesh['mem'=32,'geo'=16] {'mem'}, dimensions={0} | all-to-all | bytes 294912 | tf_op jit(solution)/shard_map/all_to_all | solution.py:232
  42.2 0.6 %member_sum.1 = f32[2,1,1152]{2,1,0:T(1,128)} custom-call(bf16[32,2,1152]{2,1,0:T(2,128)(2,1)S(1)} %all_to_all.11.terms_ref), custom_call_target="tpu_custom_call" | custom-call | tf_op jit(solution)/shard_map/member_sum/pallas_call | solution.py:214
Async XLA Ops:
  0.0 19.9 %copy-start = (bf16[2,1,32,1152]{3,2,1,0:T(8,128)(2,1)S(1)}, bf16[2,1,32,1152]{3,2,1,0:T(8,128)(2,1)}, u32[]{:S(2)}) copy-start(bf16[2,1,32,1152]{3,2,1,0:T(8,128)(2,1)} %pert_ref.1) | copy-start | bytes 442372

commit v3 on v2

--- a/solution.py
+++ b/solution.py
@@ -1,3 +1,5 @@
+import functools
+
 import jax
 import jax.numpy as jnp
 from jax import lax
@@ -7,9 +9,24 @@
 
 ITERS = 10
 LANES = 128
+GEO_FIRST = 8
+MEM_FIRST = 18
 HBM = pl.BlockSpec(memory_space=pltpu.HBM)
 VMEM = pl.BlockSpec(memory_space=pltpu.VMEM)
 SMALL = pltpu.CompilerParams(vmem_limit_bytes=4 << 20)
+
+
+def group_order(size, first):
+    return [(first + place) % size for place in range(size)]
+
+
+def store_turned(out_ref, value, first, *where):
+    rows = value.shape[0]
+    value = value.astype(out_ref.dtype)
+    for start, stop in ((first, rows), (0, first)):
+        if stop > start:
+            place = (start - first) % rows
+            out_ref[(slice(place, place + stop - start), *where)] = value[start:stop]
 
 
 def coefficients(bounds_ref, bands_ref, out_ref):
@@ -35,6 +52,7 @@
 
 
 def diffuse_kernel(
+    first,
     control_hbm,
     table_hbm,
     index_hbm,
@@ -134,11 +152,11 @@
         states = [step(state) for state in states]
     for level in range(levels):
         for r in each:
-            value = states[level][r].astype(jnp.bfloat16)
-            out_ref[:, level, r * width : (r + 1) * width] = value
-
-
-def diffuse(control, table, index, bounds, bands, groups):
+            lanes = slice(r * width, (r + 1) * width)
+            store_turned(out_ref, states[level][r], first, level, lanes)
+
+
+def diffuse(control, table, index, bounds, bands, groups, first):
     levels, height, width = control.shape[1:]
     share = height * width // groups
     arguments = [
@@ -146,7 +164,7 @@
         for x in (control, table, index, bounds, bands)
     ]
     return pl.pallas_call(
-        diffuse_kernel,
+        functools.partial(diffuse_kernel, first),
         out_shape=(
             jax.ShapeDtypeStruct((groups, levels, share), jnp.bfloat16),
             jax.ShapeDtypeStruct((bands.shape[0], bands.shape[2], share), jnp.float32),
@@ -167,7 +185,7 @@
     )(*arguments)
 
 
-def product_kernel(state_ref, coef_ref, pert_ref, out_ref, pad_ref):
+def product_kernel(geo_first, mem_first, state_ref, coef_ref, pert_ref, out_ref, pad_ref):
     shards, share, width = state_ref.shape
     levels = shards * share
     bands = coef_ref.shape[0]
@@ -176,23 +194,23 @@
         lanes = slice(c * LANES, (c + 1) * LANES)
         pad_ref[c, 0:margin] = jnp.zeros((margin, LANES), jnp.float32)
         pad_ref[c, margin + levels : 2 * margin + levels] = jnp.zeros((margin, LANES), jnp.float32)
-        for g in range(shards):
+        for place, g in enumerate(group_order(shards, geo_first)):
             rows = slice(margin + g * share, margin + (g + 1) * share)
-            pad_ref[c, rows] = state_ref[g, :, lanes].astype(jnp.float32)
+            pad_ref[c, rows] = state_ref[place, :, lanes].astype(jnp.float32)
         value = pad_ref[c, margin : margin + levels]
         for k in range(bands):
             start = margin + k - bands // 2
             value = value + coef_ref[k, :, lanes] * pad_ref[c, start : start + levels]
         for v in range(2):
             product = pert_ref[v, 0, :, lanes].astype(jnp.float32) * value
-            out_ref[:, v, lanes] = product.astype(jnp.bfloat16)
-
-
-def products(state, coefs, perturbation):
+            store_turned(out_ref, product, mem_first, v, lanes)
+
+
+def products(state, coefs, perturbation, geo_first, mem_first):
     shards, share, width = state.shape
     levels = shards * share
     return pl.pallas_call(
-        product_kernel,
+        functools.partial(product_kernel, geo_first, mem_first),
         out_shape=jax.ShapeDtypeStruct((levels, 2, width), jnp.bfloat16),
         in_specs=[VMEM, VMEM, VMEM],
         out_specs=VMEM,
@@ -221,15 +239,23 @@
     )(terms)
 
 
+def exchange(x, axis, size, first):
+    order = group_order(size, first)
+    return lax.all_to_all(x, axis, 0, 0, axis_index_groups=[order], tiled=True)
+
+
 def solution(mesh):
-    groups = mesh.shape["geo"]
+    groups, members = mesh.shape["geo"], mesh.shape["mem"]
+    geo_first, mem_first = GEO_FIRST % groups, MEM_FIRST % members
 
     def body(control, kappa_table, kappa_index, tile_bounds, filter_bands, perturbation):
         bands = jnp.transpose(filter_bands, (1, 0, 2))
-        sent, coefs = diffuse(control, kappa_table, kappa_index, tile_bounds, bands, groups)
-        state = lax.all_to_all(sent, "geo", 0, 0, tiled=True)
-        terms = products(state, coefs, perturbation)
-        return member_sum(lax.all_to_all(terms, "mem", 0, 0, tiled=True))
+        sent, coefs = diffuse(
+            control, kappa_table, kappa_index, tile_bounds, bands, groups, geo_first
+        )
+        state = exchange(sent, "geo", groups, geo_first)
+        terms = products(state, coefs, perturbation, geo_first, mem_first)
+        return member_sum(exchange(terms, "mem", members, mem_first))
 
     in_specs = (P("mem", "geo", None, None), P(), P(), P(), P(), P(None, "mem", None, "geo"))
     out_specs = P(None, "mem", "geo")

time: 43.1 us -> 36.8 us (0.85)
  blocking collectives: 39.2 us -> 33 us
    all_to_all x2, blocking collectives: 39.2 us -> 33 us  [exchange(): return lax.all_to_all(x, axis, 0, 0, axis_index_groups=[order], tiled=True)]
where the time goes in v3:
time: 36.8 us; the launch traced here: 36.6 us
  blocking collectives  33 us (90%)
  Pallas kernels  3.64 us (10%)
    all_to_all x2, blocking collectives, exchange(): return lax.all_to_all(x, axis, 0, 0, axis_index_groups=[order], tiled=True)  33 us
    pallas_call x1, Pallas kernels, diffuse(): pl.pallas_call(functools.partial(diffuse_kernel, first), out_shape=(jax.S...  2.55 us

profile of v3, /device:TPU:1, one launch (start us, length us, event | category | flops | bytes accessed | tf_op | source)
XLA Modules:
  0.0 36.6 jit_solution(13288684130262787624)
XLA Ops:
  0.0 0.0 copy-start
  0.0 2.6 %diffuse.1 = (bf16[16,2,1152]{2,1,0:T(2,128)(2,1)S(1)}, f32[5,32,1152]{2,1,0:T(8,128)S(1)}) custom-call(f32[1,2,48,384]{3,2,1,0:T(8,128)} %control_hbm.1, f32[16]{0:T(128)} %table_hbm.1, s32[48,384]{1,0:T(8,128)} %index_hbm.1, s32[17]{0:T(128)} %bounds_hbm.1, f32[5,16,32]{2,1,0:T(8,128)} %bitcast.1), custom_call_target="tpu_custom_call" | custom-call | tf_op jit(solution)/shard_map/diffuse/pallas_call | solution.py:166
  2.6 16.8 %all_to_all.10.state_ref = bf16[16,2,1152]{2,1,0:T(2,128)(2,1)S(1)} all-to-all(bf16[16,2,1152]{2,1,0:T(2,128)(2,1)S(1)} %get-tuple-element.7), channel_id=1, replica_groups={{8,9,10,11,12,13,14,15,0,1,2,3,4,5,6,7},{24,25,26,27,28,29,30,31,16,17,..., dimensions={0} | all-to-all | bytes 147456 | tf_op jit(solution)/shard_map/all_to_all | solution.py:244
  19.4 0.0 copy-done
  19.4 0.4 %products.1 = bf16[32,2,1152]{2,1,0:T(2,128)(2,1)S(1)} custom-call(bf16[16,2,1152]{2,1,0:T(2,128)(2,1)S(1)} %all_to_all.10.state_ref, f32[5,32,1152]{2,1,0:T(8,128)S(1)} %get-tuple-element.8.coef_ref, bf16[2,1,32,1152]{3,2,1,0:T(8,128)(2,1)S(1)} %copy-done), custom_call_target="tpu_custom_call" | custom-call | tf_op jit(solution)/shard_map/products/pallas_call | solution.py:212
  19.8 16.2 %all_to_all.11.terms_ref = bf16[32,2,1152]{2,1,0:T(2,128)(2,1)S(1)} all-to-all(bf16[32,2,1152]{2,1,0:T(2,128)(2,1)S(1)} %products.1), channel_id=1, replica_groups={{288,304,320,336,352,368,384,400,416,432,448,464,480,496,0,16,32,48,64,..., dimensions={0} | all-to-all | bytes 294912 | tf_op jit(solution)/shard_map/all_to_all | solution.py:244
  36.0 0.6 %member_sum.1 = f32[2,1,1152]{2,1,0:T(1,128)} custom-call(bf16[32,2,1152]{2,1,0:T(2,128)(2,1)S(1)} %all_to_all.11.terms_ref), custom_call_target="tpu_custom_call" | custom-call | tf_op jit(solution)/shard_map/member_sum/pallas_call | solution.py:232
Async XLA Ops:
  0.0 19.4 %copy-start = (bf16[2,1,32,1152]{3,2,1,0:T(8,128)(2,1)S(1)}, bf16[2,1,32,1152]{3,2,1,0:T(8,128)(2,1)}, u32[]{:S(2)}) copy-start(bf16[2,1,32,1152]{3,2,1,0:T(8,128)(2,1)} %pert_ref.1) | copy-start | bytes 442372

commit v4 on v2

--- a/solution.py
+++ b/solution.py
@@ -1,3 +1,5 @@
+import functools
+
 import jax
 import jax.numpy as jnp
 from jax import lax
@@ -7,9 +9,21 @@
 
 ITERS = 10
 LANES = 128
+GEO_FIRST = 9
+MEM_FIRST = 26
 HBM = pl.BlockSpec(memory_space=pltpu.HBM)
 VMEM = pl.BlockSpec(memory_space=pltpu.VMEM)
 SMALL = pltpu.CompilerParams(vmem_limit_bytes=4 << 20)
+
+
+def group_order(size, first):
+    return [(first - place) % size for place in range(size)]
+
+
+def store_ordered(out_ref, value, order, *where):
+    value = value.astype(out_ref.dtype)
+    for place, row in enumerate(order):
+        out_ref[(place, *where)] = value[row]
 
 
 def coefficients(bounds_ref, bands_ref, out_ref):
@@ -35,6 +49,7 @@
 
 
 def diffuse_kernel(
+    order,
     control_hbm,
     table_hbm,
     index_hbm,
@@ -103,9 +118,6 @@
     def previous_group(x):
         return pltpu.roll(x, 1, 0)
 
-    copies[0].wait()
-    copies[1].wait()
-    coefficients(bounds_ref, bands_ref, coef_ref)
     copies[2].wait()
     copies[3].wait()
     kappa = split(levels, kappa_of)
@@ -129,24 +141,28 @@
         ]
 
     copies[4].wait()
+    copies[0].wait()
+    copies[1].wait()
+    coefficients(bounds_ref, bands_ref, coef_ref)
     states = [split(v, lambda lanes: control_ref[0, v, :, lanes]) for v in range(levels)]
     for _ in range(ITERS):
         states = [step(state) for state in states]
     for level in range(levels):
         for r in each:
-            value = states[level][r].astype(jnp.bfloat16)
-            out_ref[:, level, r * width : (r + 1) * width] = value
-
-
-def diffuse(control, table, index, bounds, bands, groups):
+            lanes = slice(r * width, (r + 1) * width)
+            store_ordered(out_ref, states[level][r], order, level, lanes)
+
+
+def diffuse(control, table, index, bounds, bands, order):
     levels, height, width = control.shape[1:]
+    groups = len(order)
     share = height * width // groups
     arguments = [
         pltpu.with_memory_space_constraint(x, pltpu.HBM)
         for x in (control, table, index, bounds, bands)
     ]
     return pl.pallas_call(
-        diffuse_kernel,
+        functools.partial(diffuse_kernel, order),
         out_shape=(
             jax.ShapeDtypeStruct((groups, levels, share), jnp.bfloat16),
             jax.ShapeDtypeStruct((bands.shape[0], bands.shape[2], share), jnp.float32),
@@ -167,7 +183,7 @@
     )(*arguments)
 
 
-def product_kernel(state_ref, coef_ref, pert_ref, out_ref, pad_ref):
+def product_kernel(geo_order, mem_order, state_ref, coef_ref, pert_ref, out_ref, pad_ref):
     shards, share, width = state_ref.shape
     levels = shards * share
     bands = coef_ref.shape[0]
@@ -176,23 +192,23 @@
         lanes = slice(c * LANES, (c + 1) * LANES)
         pad_ref[c, 0:margin] = jnp.zeros((margin, LANES), jnp.float32)
         pad_ref[c, margin + levels : 2 * margin + levels] = jnp.zeros((margin, LANES), jnp.float32)
-        for g in range(shards):
+        for place, g in enumerate(geo_order):
             rows = slice(margin + g * share, margin + (g + 1) * share)
-            pad_ref[c, rows] = state_ref[g, :, lanes].astype(jnp.float32)
+            pad_ref[c, rows] = state_ref[place, :, lanes].astype(jnp.float32)
         value = pad_ref[c, margin : margin + levels]
         for k in range(bands):
             start = margin + k - bands // 2
             value = value + coef_ref[k, :, lanes] * pad_ref[c, start : start + levels]
         for v in range(2):
             product = pert_ref[v, 0, :, lanes].astype(jnp.float32) * value
-            out_ref[:, v, lanes] = product.astype(jnp.bfloat16)
-
-
-def products(state, coefs, perturbation):
+            store_ordered(out_ref, product, mem_order, v, lanes)
+
+
+def products(state, coefs, perturbation, geo_order, mem_order):
     shards, share, width = state.shape
     levels = shards * share
     return pl.pallas_call(
-        product_kernel,
+        functools.partial(product_kernel, geo_order, mem_order),
         out_shape=jax.ShapeDtypeStruct((levels, 2, width), jnp.bfloat16),
         in_specs=[VMEM, VMEM, VMEM],
         out_specs=VMEM,
@@ -221,15 +237,20 @@
     )(terms)
 
 
+def exchange(x, axis, order):
+    return lax.all_to_all(x, axis, 0, 0, axis_index_groups=[order], tiled=True)
+
+
 def solution(mesh):
-    groups = mesh.shape["geo"]
+    geo_order = group_order(mesh.shape["geo"], GEO_FIRST % mesh.shape["geo"])
+    mem_order = group_order(mesh.shape["mem"], MEM_FIRST % mesh.shape["mem"])
 
     def body(control, kappa_table, kappa_index, tile_bounds, filter_bands, perturbation):
         bands = jnp.transpose(filter_bands, (1, 0, 2))
-        sent, coefs = diffuse(control, kappa_table, kappa_index, tile_bounds, bands, groups)
-        state = lax.all_to_all(sent, "geo", 0, 0, tiled=True)
-        terms = products(state, coefs, perturbation)
-        return member_sum(lax.all_to_all(terms, "mem", 0, 0, tiled=True))
+        sent, coefs = diffuse(control, kappa_table, kappa_index, tile_bounds, bands, geo_order)
+        state = exchange(sent, "geo", geo_order)
+        terms = products(state, coefs, perturbation, geo_order, mem_order)
+        return member_sum(exchange(terms, "mem", mem_order))
 
     in_specs = (P("mem", "geo", None, None), P(), P(), P(), P(), P(None, "mem", None, "geo"))
     out_specs = P(None, "mem", "geo")

time: 43.1 us -> 34.7 us (0.81)
  blocking collectives: 39.2 us -> 30.8 us
    all_to_all x2, blocking collectives: 39.2 us -> 30.8 us  [exchange(): return lax.all_to_all(x, axis, 0, 0, axis_index_groups=[order], tiled=True)]
where the time goes in v4:
time: 34.7 us; the launch traced here: 34.1 us
  blocking collectives  30.8 us (89%)
  Pallas kernels  3.32 us (10%)
    all_to_all x2, blocking collectives, exchange(): return lax.all_to_all(x, axis, 0, 0, axis_index_groups=[order], tiled=True)  30.8 us
    pallas_call x1, Pallas kernels, diffuse(): pl.pallas_call(functools.partial(diffuse_kernel, order), out_shape=(jax.S...  2.28 us

profile of v4, /device:TPU:1, one launch (start us, length us, event | category | flops | bytes accessed | tf_op | source)
XLA Modules:
  0.0 34.1 jit_solution(32321401997412692)
XLA Ops:
  0.0 0.0 copy-start
  0.0 2.3 %diffuse.1 = (bf16[16,2,1152]{2,1,0:T(2,128)(2,1)S(1)}, f32[5,32,1152]{2,1,0:T(8,128)S(1)}) custom-call(f32[1,2,48,384]{3,2,1,0:T(8,128)} %control_hbm.1, f32[16]{0:T(128)} %table_hbm.1, s32[48,384]{1,0:T(8,128)} %index_hbm.1, s32[17]{0:T(128)} %bounds_hbm.1, f32[5,16,32]{2,1,0:T(8,128)} %bitcast.1), custom_call_target="tpu_custom_call" | custom-call | tf_op jit(solution)/shard_map/diffuse/pallas_call | solution.py:164
  2.3 16.1 %all_to_all.10.state_ref = bf16[16,2,1152]{2,1,0:T(2,128)(2,1)S(1)} all-to-all(bf16[16,2,1152]{2,1,0:T(2,128)(2,1)S(1)} %get-tuple-element.7), channel_id=1, replica_groups={{9,8,7,6,5,4,3,2,1,0,15,14,13,12,11,10},{25,24,23,22,21,20,19,18,17,16,..., dimensions={0} | all-to-all | bytes 147456 | tf_op jit(solution)/shard_map/all_to_all | solution.py:241
  18.4 0.0 copy-done
  18.4 0.4 %products.1 = bf16[32,2,1152]{2,1,0:T(2,128)(2,1)S(1)} custom-call(bf16[16,2,1152]{2,1,0:T(2,128)(2,1)S(1)} %all_to_all.10.state_ref, f32[5,32,1152]{2,1,0:T(8,128)S(1)} %get-tuple-element.8.coef_ref, bf16[2,1,32,1152]{3,2,1,0:T(8,128)(2,1)S(1)} %copy-done), custom_call_target="tpu_custom_call" | custom-call | tf_op jit(solution)/shard_map/products/pallas_call | solution.py:210
  18.8 14.7 %all_to_all.11.terms_ref = bf16[32,2,1152]{2,1,0:T(2,128)(2,1)S(1)} all-to-all(bf16[32,2,1152]{2,1,0:T(2,128)(2,1)S(1)} %products.1), channel_id=1, replica_groups={{416,400,384,368,352,336,320,304,288,272,256,240,224,208,192,176,160,14..., dimensions={0} | all-to-all | bytes 294912 | tf_op jit(solution)/shard_map/all_to_all | solution.py:241
  33.5 0.6 %member_sum.1 = f32[2,1,1152]{2,1,0:T(1,128)} custom-call(bf16[32,2,1152]{2,1,0:T(2,128)(2,1)S(1)} %all_to_all.11.terms_ref), custom_call_target="tpu_custom_call" | custom-call | tf_op jit(solution)/shard_map/member_sum/pallas_call | solution.py:230
Async XLA Ops:
  0.0 18.4 %copy-start = (bf16[2,1,32,1152]{3,2,1,0:T(8,128)(2,1)S(1)}, bf16[2,1,32,1152]{3,2,1,0:T(8,128)(2,1)}, u32[]{:S(2)}) copy-start(bf16[2,1,32,1152]{3,2,1,0:T(8,128)(2,1)} %pert_ref.1) | copy-start | bytes 442372

commit v5 on v4

--- a/solution.py
+++ b/solution.py
@@ -69,11 +69,11 @@
         pltpu.make_async_copy(source, target, sems.at[i])
         for i, (source, target) in enumerate(
             (
+                (index_hbm, index_ref),
+                (table_hbm, table_ref),
+                (control_hbm, control_ref),
                 (bounds_hbm, bounds_ref),
                 (bands_hbm, bands_ref),
-                (table_hbm, table_ref),
-                (index_hbm, index_ref),
-                (control_hbm, control_ref),
             )
         )
     ]
@@ -118,8 +118,8 @@
     def previous_group(x):
         return pltpu.roll(x, 1, 0)
 
-    copies[2].wait()
-    copies[3].wait()
+    copies[1].wait()
+    copies[0].wait()
     kappa = split(levels, kappa_of)
     column = lax.broadcasted_iota(jnp.int32, (groups, width), 1)
     group = lax.broadcasted_iota(jnp.int32, (groups, width), 0)
@@ -140,9 +140,9 @@
             for r in each
         ]
 
+    copies[2].wait()
+    copies[3].wait()
     copies[4].wait()
-    copies[0].wait()
-    copies[1].wait()
     coefficients(bounds_ref, bands_ref, coef_ref)
     states = [split(v, lambda lanes: control_ref[0, v, :, lanes]) for v in range(levels)]
     for _ in range(ITERS):
@@ -183,7 +183,7 @@
     )(*arguments)
 
 
-def product_kernel(geo_order, mem_order, state_ref, coef_ref, pert_ref, out_ref, pad_ref):
+def product_kernel(geo_order, mem_order, state_ref, coef_ref, pert_ref, out_ref, pad_ref, pair_ref):
     shards, share, width = state_ref.shape
     levels = shards * share
     bands = coef_ref.shape[0]
@@ -201,7 +201,10 @@
             value = value + coef_ref[k, :, lanes] * pad_ref[c, start : start + levels]
         for v in range(2):
             product = pert_ref[v, 0, :, lanes].astype(jnp.float32) * value
-            store_ordered(out_ref, product, mem_order, v, lanes)
+            pair_ref[c, pl.ds(v, levels, stride=2), :] = product
+        for place, level in enumerate(mem_order):
+            pair = pair_ref[c, 2 * level : 2 * level + 2]
+            out_ref[place, :, lanes] = pair.astype(jnp.bfloat16)
 
 
 def products(state, coefs, perturbation, geo_order, mem_order):
@@ -212,7 +215,10 @@
         out_shape=jax.ShapeDtypeStruct((levels, 2, width), jnp.bfloat16),
         in_specs=[VMEM, VMEM, VMEM],
         out_specs=VMEM,
-        scratch_shapes=[pltpu.VMEM((width // LANES, levels + 16, LANES), jnp.float32)],
+        scratch_shapes=[
+            pltpu.VMEM((width // LANES, levels + 16, LANES), jnp.float32),
+            pltpu.VMEM((width // LANES, 2 * levels, LANES), jnp.float32),
+        ],
         compiler_params=SMALL,
         name="products",
     )(state, coefs, perturbation)

time: 34.7 us -> 34.6 us (level)
  no operation moved by 1% of the time
where the time goes in v5:
time: 34.6 us; the launch traced here: 34 us
  blocking collectives  30.8 us (89%)
  Pallas kernels  3.18 us (9%)
    all_to_all x2, blocking collectives, exchange(): return lax.all_to_all(x, axis, 0, 0, axis_index_groups=[order], tiled=True)  30.8 us
    pallas_call x1, Pallas kernels, diffuse(): pl.pallas_call(functools.partial(diffuse_kernel, order), out_shape=(jax.S...  2.26 us

profile of v5, /device:TPU:1, one launch (start us, length us, event | category | flops | bytes accessed | tf_op | source)
XLA Modules:
  0.0 34.0 jit_solution(10663357996327462470)
XLA Ops:
  0.0 0.0 copy-start
  0.0 2.3 %diffuse.1 = (bf16[16,2,1152]{2,1,0:T(2,128)(2,1)S(1)}, f32[5,32,1152]{2,1,0:T(8,128)S(1)}) custom-call(f32[1,2,48,384]{3,2,1,0:T(8,128)} %control_hbm.1, f32[16]{0:T(128)} %table_hbm.1, s32[48,384]{1,0:T(8,128)} %index_hbm.1, s32[17]{0:T(128)} %bounds_hbm.1, f32[5,16,32]{2,1,0:T(8,128)} %bitcast.1), custom_call_target="tpu_custom_call" | custom-call | tf_op jit(solution)/shard_map/diffuse/pallas_call | solution.py:164
  2.3 16.1 %all_to_all.10.state_ref = bf16[16,2,1152]{2,1,0:T(2,128)(2,1)S(1)} all-to-all(bf16[16,2,1152]{2,1,0:T(2,128)(2,1)S(1)} %get-tuple-element.7), channel_id=1, replica_groups={{9,8,7,6,5,4,3,2,1,0,15,14,13,12,11,10},{25,24,23,22,21,20,19,18,17,16,..., dimensions={0} | all-to-all | bytes 147456 | tf_op jit(solution)/shard_map/all_to_all | solution.py:247
  18.4 0.0 copy-done
  18.4 0.3 products.1
  18.7 14.7 %all_to_all.11.terms_ref = bf16[32,2,1152]{2,1,0:T(2,128)(2,1)S(1)} all-to-all(bf16[32,2,1152]{2,1,0:T(2,128)(2,1)S(1)} %products.1), channel_id=1, replica_groups={{416,400,384,368,352,336,320,304,288,272,256,240,224,208,192,176,160,14..., dimensions={0} | all-to-all | bytes 294912 | tf_op jit(solution)/shard_map/all_to_all | solution.py:247
  33.4 0.6 %member_sum.1 = f32[2,1,1152]{2,1,0:T(1,128)} custom-call(bf16[32,2,1152]{2,1,0:T(2,128)(2,1)S(1)} %all_to_all.11.terms_ref), custom_call_target="tpu_custom_call" | custom-call | tf_op jit(solution)/shard_map/member_sum/pallas_call | solution.py:236
Async XLA Ops:
  0.0 18.4 %copy-start = (bf16[2,1,32,1152]{3,2,1,0:T(8,128)(2,1)S(1)}, bf16[2,1,32,1152]{3,2,1,0:T(8,128)(2,1)}, u32[]{:S(2)}) copy-start(bf16[2,1,32,1152]{3,2,1,0:T(8,128)(2,1)} %pert_ref.1) | copy-start | bytes 442372

commit v6 on v5

--- a/solution.py
+++ b/solution.py
@@ -9,6 +9,7 @@
 
 ITERS = 10
 LANES = 128
+SUBLANES = 8
 GEO_FIRST = 9
 MEM_FIRST = 26
 HBM = pl.BlockSpec(memory_space=pltpu.HBM)
@@ -18,12 +19,6 @@
 
 def group_order(size, first):
     return [(first - place) % size for place in range(size)]
-
-
-def store_ordered(out_ref, value, order, *where):
-    value = value.astype(out_ref.dtype)
-    for place, row in enumerate(order):
-        out_ref[(place, *where)] = value[row]
 
 
 def coefficients(bounds_ref, bands_ref, out_ref):
@@ -63,6 +58,7 @@
     bounds_ref,
     bands_ref,
     rows_ref,
+    pair_ref,
     sems,
 ):
     copies = [
@@ -80,8 +76,9 @@
     for copy in copies:
         copy.start()
     levels, height, width = control_ref.shape[1:]
-    groups = out_ref.shape[0]
+    groups = SUBLANES
     phases = height // groups
+    band = height // out_ref.shape[0]
     tiles = width // LANES
     each = range(phases)
 
@@ -147,10 +144,20 @@
     states = [split(v, lambda lanes: control_ref[0, v, :, lanes]) for v in range(levels)]
     for _ in range(ITERS):
         states = [step(state) for state in states]
-    for level in range(levels):
-        for r in each:
-            lanes = slice(r * width, (r + 1) * width)
-            store_ordered(out_ref, states[level][r], order, level, lanes)
+    share = phases // band
+    for r in each:
+        for k in range(tiles):
+            for v in range(levels):
+                piece = states[v][r][:, k * LANES : (k + 1) * LANES]
+                pair_ref[r, k, pl.ds(v, groups, stride=levels), :] = piece
+    for r in each:
+        for k in range(tiles):
+            start = r % band * width + k * LANES
+            lanes = slice(start, start + LANES)
+            for g in range(groups):
+                pair = pair_ref[r, k, g * levels : (g + 1) * levels]
+                place = order.index(g * share + r // band)
+                out_ref[place, :, lanes] = pair.astype(jnp.bfloat16)
 
 
 def diffuse(control, table, index, bounds, bands, order):
@@ -176,6 +183,7 @@
             pltpu.SMEM(bounds.shape, jnp.int32),
             pltpu.VMEM(bands.shape, jnp.float32),
             pltpu.VMEM((levels + 1, width // LANES, height, LANES), jnp.float32),
+            pltpu.VMEM((height // SUBLANES, width // LANES, SUBLANES * levels, LANES), jnp.float32),
             pltpu.SemaphoreType.DMA((5,)),
         ],
         compiler_params=SMALL,

time: 34.6 us -> 34.5 us (level)
  no operation moved by 1% of the time
where the time goes in v6:
time: 34.5 us; the launch traced here: 33.9 us
  blocking collectives  30.8 us (89%)
  Pallas kernels  3.11 us (9%)
    all_to_all x2, blocking collectives, exchange(): return lax.all_to_all(x, axis, 0, 0, axis_index_groups=[order], tiled=True)  30.8 us
    pallas_call x1, Pallas kernels, diffuse(): pl.pallas_call(functools.partial(diffuse_kernel, order), out_shape=(jax.S...  2.19 us

profile of v6, /device:TPU:1, one launch (start us, length us, event | category | flops | bytes accessed | tf_op | source)
XLA Modules:
  0.0 33.9 jit_solution(7534796527029345646)
XLA Ops:
  0.0 0.0 copy-start
  0.0 2.2 %diffuse.1 = (bf16[16,2,1152]{2,1,0:T(2,128)(2,1)S(1)}, f32[5,32,1152]{2,1,0:T(8,128)S(1)}) custom-call(f32[1,2,48,384]{3,2,1,0:T(8,128)} %control_hbm.1, f32[16]{0:T(128)} %table_hbm.1, s32[48,384]{1,0:T(8,128)} %index_hbm.1, s32[17]{0:T(128)} %bounds_hbm.1, f32[5,16,32]{2,1,0:T(8,128)} %bitcast.1), custom_call_target="tpu_custom_call" | custom-call | tf_op jit(solution)/shard_map/diffuse/pallas_call | solution.py:171
  2.2 16.1 %all_to_all.10.state_ref = bf16[16,2,1152]{2,1,0:T(2,128)(2,1)S(1)} all-to-all(bf16[16,2,1152]{2,1,0:T(2,128)(2,1)S(1)} %get-tuple-element.7), channel_id=1, replica_groups={{9,8,7,6,5,4,3,2,1,0,15,14,13,12,11,10},{25,24,23,22,21,20,19,18,17,16,..., dimensions={0} | all-to-all | bytes 147456 | tf_op jit(solution)/shard_map/all_to_all | solution.py:255
  18.3 0.0 copy-done
  18.3 0.3 products.1
  18.6 14.7 %all_to_all.11.terms_ref = bf16[32,2,1152]{2,1,0:T(2,128)(2,1)S(1)} all-to-all(bf16[32,2,1152]{2,1,0:T(2,128)(2,1)S(1)} %products.1), channel_id=1, replica_groups={{416,400,384,368,352,336,320,304,288,272,256,240,224,208,192,176,160,14..., dimensions={0} | all-to-all | bytes 294912 | tf_op jit(solution)/shard_map/all_to_all | solution.py:255
  33.3 0.6 %member_sum.1 = f32[2,1,1152]{2,1,0:T(1,128)} custom-call(bf16[32,2,1152]{2,1,0:T(2,128)(2,1)S(1)} %all_to_all.11.terms_ref), custom_call_target="tpu_custom_call" | custom-call | tf_op jit(solution)/shard_map/member_sum/pallas_call | solution.py:244
Async XLA Ops:
  0.0 18.3 %copy-start = (bf16[2,1,32,1152]{3,2,1,0:T(8,128)(2,1)S(1)}, bf16[2,1,32,1152]{3,2,1,0:T(8,128)(2,1)}, u32[]{:S(2)}) copy-start(bf16[2,1,32,1152]{3,2,1,0:T(8,128)(2,1)} %pert_ref.1) | copy-start | bytes 442372

commit v7 on v6

--- a/solution.py
+++ b/solution.py
@@ -50,8 +50,10 @@
     index_hbm,
     bounds_hbm,
     bands_hbm,
+    pert_hbm,
     out_ref,
     coef_ref,
+    pert_ref,
     control_ref,
     table_ref,
     index_ref,
@@ -138,6 +140,8 @@
         ]
 
     copies[2].wait()
+    pert_copy = pltpu.make_async_copy(pert_hbm, pert_ref, sems.at[5])
+    pert_copy.start()
     copies[3].wait()
     copies[4].wait()
     coefficients(bounds_ref, bands_ref, coef_ref)
@@ -158,24 +162,26 @@
                 pair = pair_ref[r, k, g * levels : (g + 1) * levels]
                 place = order.index(g * share + r // band)
                 out_ref[place, :, lanes] = pair.astype(jnp.bfloat16)
-
-
-def diffuse(control, table, index, bounds, bands, order):
+    pert_copy.wait()
+
+
+def diffuse(control, table, index, bounds, bands, perturbation, order):
     levels, height, width = control.shape[1:]
     groups = len(order)
     share = height * width // groups
     arguments = [
         pltpu.with_memory_space_constraint(x, pltpu.HBM)
-        for x in (control, table, index, bounds, bands)
+        for x in (control, table, index, bounds, bands, perturbation)
     ]
     return pl.pallas_call(
         functools.partial(diffuse_kernel, order),
         out_shape=(
             jax.ShapeDtypeStruct((groups, levels, share), jnp.bfloat16),
             jax.ShapeDtypeStruct((bands.shape[0], bands.shape[2], share), jnp.float32),
+            jax.ShapeDtypeStruct(perturbation.shape, perturbation.dtype),
         ),
-        in_specs=[HBM] * 5,
-        out_specs=(VMEM, VMEM),
+        in_specs=[HBM] * 6,
+        out_specs=(VMEM, VMEM, VMEM),
         scratch_shapes=[
             pltpu.VMEM(control.shape, jnp.float32),
             pltpu.SMEM(table.shape, jnp.float32),
@@ -184,7 +190,7 @@
             pltpu.VMEM(bands.shape, jnp.float32),
             pltpu.VMEM((levels + 1, width // LANES, height, LANES), jnp.float32),
             pltpu.VMEM((height // SUBLANES, width // LANES, SUBLANES * levels, LANES), jnp.float32),
-            pltpu.SemaphoreType.DMA((5,)),
+            pltpu.SemaphoreType.DMA((6,)),
         ],
         compiler_params=SMALL,
         name="diffuse",
@@ -261,9 +267,11 @@
 
     def body(control, kappa_table, kappa_index, tile_bounds, filter_bands, perturbation):
         bands = jnp.transpose(filter_bands, (1, 0, 2))
-        sent, coefs = diffuse(control, kappa_table, kappa_index, tile_bounds, bands, geo_order)
+        sent, coefs, pert = diffuse(
+            control, kappa_table, kappa_index, tile_bounds, bands, perturbation, geo_order
+        )
         state = exchange(sent, "geo", geo_order)
-        terms = products(state, coefs, perturbation, geo_order, mem_order)
+        terms = products(state, coefs, pert, geo_order, mem_order)
         return member_sum(exchange(terms, "mem", mem_order))
 
     in_specs = (P("mem", "geo", None, None), P(), P(), P(), P(), P(None, "mem", None, "geo"))

time: 34.5 us -> 34.5 us (level)
  no operation moved by 1% of the time
where the time goes in v7:
time: 34.5 us; the launch traced here: 33.9 us
  blocking collectives  30.8 us (89%)
  Pallas kernels  3.08 us (9%)
    all_to_all x2, blocking collectives, exchange(): return lax.all_to_all(x, axis, 0, 0, axis_index_groups=[order], tiled=True)  30.8 us
    pallas_call x1, Pallas kernels, diffuse(): pl.pallas_call(functools.partial(diffuse_kernel, order), out_shape=(jax.S...  2.16 us

profile of v7, /device:TPU:1, one launch (start us, length us, event | category | flops | bytes accessed | tf_op | source)
XLA Modules:
  0.0 33.9 jit_solution(7446324600782190976)
XLA Ops:
  0.0 2.2 %diffuse.1 = (bf16[16,2,1152]{2,1,0:T(2,128)(2,1)S(1)}, f32[5,32,1152]{2,1,0:T(8,128)S(1)}, bf16[2,1,32,1152]{3,2,1,0:T(8,128)(2,1)S(1)}) custom-call(f32[1,2,48,384]{3,2,1,0:T(8,128)} %control_hbm.1, f32[16]{0:T(128)} %table_hbm.1, s32[48,384]{1,0:T(8,128)} %index_hbm.1, s32[17]{0:T(128)} %bounds_hbm.1, f32[5,16,32]{2,1,0:T(8,128)} %bitcast.1, ...), custom_call_target="tpu_custom_call" | custom-call | tf_op jit(solution)/shard_map/diffuse/pallas_call | solution.py:176
  2.2 16.1 %all_to_all.10.state_ref = bf16[16,2,1152]{2,1,0:T(2,128)(2,1)S(1)} all-to-all(bf16[16,2,1152]{2,1,0:T(2,128)(2,1)S(1)} %get-tuple-element.8), channel_id=1, replica_groups={{9,8,7,6,5,4,3,2,1,0,15,14,13,12,11,10},{25,24,23,22,21,20,19,18,17,16,..., dimensions={0} | all-to-all | bytes 147456 | tf_op jit(solution)/shard_map/all_to_all | solution.py:261
  18.3 0.3 products.1
  18.6 14.7 %all_to_all.11.terms_ref = bf16[32,2,1152]{2,1,0:T(2,128)(2,1)S(1)} all-to-all(bf16[32,2,1152]{2,1,0:T(2,128)(2,1)S(1)} %products.1), channel_id=1, replica_groups={{416,400,384,368,352,336,320,304,288,272,256,240,224,208,192,176,160,14..., dimensions={0} | all-to-all | bytes 294912 | tf_op jit(solution)/shard_map/all_to_all | solution.py:261
  33.3 0.6 %member_sum.1 = f32[2,1,1152]{2,1,0:T(1,128)} custom-call(bf16[32,2,1152]{2,1,0:T(2,128)(2,1)S(1)} %all_to_all.11.terms_ref), custom_call_target="tpu_custom_call" | custom-call | tf_op jit(solution)/shard_map/member_sum/pallas_call | solution.py:250

commit v8 on v7

--- a/solution.py
+++ b/solution.py
@@ -239,9 +239,11 @@
 
 
 def sum_kernel(terms_ref, out_ref):
-    total = terms_ref[0].astype(jnp.float32)
-    for m in range(1, terms_ref.shape[0]):
-        total = total + terms_ref[m].astype(jnp.float32)
+    members = terms_ref.shape[0]
+    chains = [terms_ref[m].astype(jnp.float32) for m in range(4)]
+    for m in range(4, members):
+        chains[m % 4] = chains[m % 4] + terms_ref[m].astype(jnp.float32)
+    total = (chains[0] + chains[1]) + (chains[2] + chains[3])
     for v in range(2):
         out_ref[v] = total[v : v + 1]
 

time: 34.5 us -> 34.5 us (level)
  no operation moved by 1% of the time
where the time goes in v8:
time: 34.5 us; the launch traced here: 33.9 us
  blocking collectives  30.8 us (89%)
  Pallas kernels  3.07 us (9%)
    all_to_all x2, blocking collectives, exchange(): return lax.all_to_all(x, axis, 0, 0, axis_index_groups=[order], tiled=True)  30.8 us
    pallas_call x1, Pallas kernels, diffuse(): pl.pallas_call(functools.partial(diffuse_kernel, order), out_shape=(jax.S...  2.16 us

profile of v8, /device:TPU:1, one launch (start us, length us, event | category | flops | bytes accessed | tf_op | source)
XLA Modules:
  0.0 33.9 jit_solution(1749915001386593683)
XLA Ops:
  0.0 2.2 %diffuse.1 = (bf16[16,2,1152]{2,1,0:T(2,128)(2,1)S(1)}, f32[5,32,1152]{2,1,0:T(8,128)S(1)}, bf16[2,1,32,1152]{3,2,1,0:T(8,128)(2,1)S(1)}) custom-call(f32[1,2,48,384]{3,2,1,0:T(8,128)} %control_hbm.1, f32[16]{0:T(128)} %table_hbm.1, s32[48,384]{1,0:T(8,128)} %index_hbm.1, s32[17]{0:T(128)} %bounds_hbm.1, f32[5,16,32]{2,1,0:T(8,128)} %bitcast.1, ...), custom_call_target="tpu_custom_call" | custom-call | tf_op jit(solution)/shard_map/diffuse/pallas_call | solution.py:176
  2.2 16.1 %all_to_all.10.state_ref = bf16[16,2,1152]{2,1,0:T(2,128)(2,1)S(1)} all-to-all(bf16[16,2,1152]{2,1,0:T(2,128)(2,1)S(1)} %get-tuple-element.8), channel_id=1, replica_groups={{9,8,7,6,5,4,3,2,1,0,15,14,13,12,11,10},{25,24,23,22,21,20,19,18,17,16,..., dimensions={0} | all-to-all | bytes 147456 | tf_op jit(solution)/shard_map/all_to_all | solution.py:263
  18.3 0.3 products.1
  18.6 14.7 %all_to_all.11.terms_ref = bf16[32,2,1152]{2,1,0:T(2,128)(2,1)S(1)} all-to-all(bf16[32,2,1152]{2,1,0:T(2,128)(2,1)S(1)} %products.1), channel_id=1, replica_groups={{416,400,384,368,352,336,320,304,288,272,256,240,224,208,192,176,160,14..., dimensions={0} | all-to-all | bytes 294912 | tf_op jit(solution)/shard_map/all_to_all | solution.py:263
  33.3 0.6 %member_sum.1 = f32[2,1,1152]{2,1,0:T(1,128)} custom-call(bf16[32,2,1152]{2,1,0:T(2,128)(2,1)S(1)} %all_to_all.11.terms_ref), custom_call_target="tpu_custom_call" | custom-call | tf_op jit(solution)/shard_map/member_sum/pallas_call | solution.py:252
